TPU v7x, 32 devices: a whole 2x2x4 slice. The times are simulated.
32 devices in a mesh: band: 2 (over y), rtile: 4 (over z), stile: 2 (over x), freq: 2 (over core).
Axes of the slice: x: 2, y: 2, z: 4, core: 2. Of those that a mesh axis runs over, the one named last changes fastest.
Arguments:
- x_start: float32 [4, 8, 2, 256, 128], P(('band', 'freq'), 'rtile', None, None, 'stile'), parts along dimension 0, may hold values from -6 to 6
- data: float32 [4, 4, 2, 2, 256, 128], P(('band', 'freq'), 'rtile', 'stile'), parts along dimension 0, may hold values from -6 to 6
- u_fac: bfloat16 [4, 4, 2, 8, 2, 64, 256], P(('band', 'freq'), 'rtile', 'stile'), parts along dimension 0, may hold values from -0.75 to 0.75
- v_fac: bfloat16 [4, 4, 2, 8, 2, 64, 256], P(('band', 'freq'), None, 'stile', 'rtile'), parts along dimension 0, may hold values from -0.125 to 0.125
- ranks: int32 [4, 4, 2, 8], P(('band', 'freq'), None, 'stile'), parts along dimension 0, may hold values from 8 to 56, as said below
- slot_tile: int32 [8], replicated, may hold values from 0 to 7, as said below
- neighbours: int32 [8, 4], replicated, may hold values from -1 to 7, as said below
Outputs:
- x_final: float32 [4, 8, 2, 256, 128], P(('band', 'freq'), 'rtile', None, None, 'stile'), parts along dimension 0
- z_final: float32 [4, 8, 2, 256, 128], P(('band', 'freq'), 'rtile', None, None, 'stile'), parts along dimension 0
There are 2 independent parts, one for each index of `band`. A program takes and returns all parts, laid end to end along the dimension named above; an argument that names none is the same for every part. Nothing has to cross between parts.
Inputs may be any that keep to these rules, and one draw needn't show every extreme that they name: Each entry is a whole multiple of one eighth of 64; for every frequency and source tile the ranks of tiles 2k and 2k+1 sum to at most 64, and for at least one frequency and source tile they sum to exactly 64. `slot_tile`: each tile appears in exactly one slot; slots 2p and 2p+1 hold the two tiles 2k and 2k+1 of one k. `neighbours`: tiles lie on a grid of four tiles a row, tile t in row t // 4; an entry is -1 or the adjacent tile in that direction, and the lists are symmetric (if tile s is east of t, t is west of s; likewise south and north).
All inputs are finite; a program needn't handle non-finite values.
Results may differ from a plain program's by a relative error of at most 0.0024.
Values may be sent and summed in bfloat16 or wider, within the bound.
A program may use at most 64 MiB of HBM per device.

v0:
```python
import jax
import jax.numpy as jnp
from jax import lax
from jax.sharding import PartitionSpec as P

EDGE = 16
RANK = 64
ITERS = 2


def conj_apply(factor, field, form):
    real = jnp.einsum(
        form, factor[..., 0, :, :], field[..., 0, :, :], preferred_element_type=jnp.float32
    )
    real = real + jnp.einsum(
        form, factor[..., 1, :, :], field[..., 1, :, :], preferred_element_type=jnp.float32
    )
    imag = jnp.einsum(
        form, factor[..., 0, :, :], field[..., 1, :, :], preferred_element_type=jnp.float32
    )
    imag = imag - jnp.einsum(
        form, factor[..., 1, :, :], field[..., 0, :, :], preferred_element_type=jnp.float32
    )
    return jnp.stack([real, imag], axis=-3)


def plain_apply(factor, panel, form):
    real = jnp.einsum(
        form, factor[..., 0, :, :], panel[..., 0, :, :], preferred_element_type=jnp.float32
    )
    real = real - jnp.einsum(
        form, factor[..., 1, :, :], panel[..., 1, :, :], preferred_element_type=jnp.float32
    )
    imag = jnp.einsum(
        form, factor[..., 0, :, :], panel[..., 1, :, :], preferred_element_type=jnp.float32
    )
    imag = imag + jnp.einsum(
        form, factor[..., 1, :, :], panel[..., 0, :, :], preferred_element_type=jnp.float32
    )
    return jnp.stack([real, imag], axis=-3)


def interior(grid):
    diff_a = grid[:, :, 1:] - grid[:, :, :-1]
    diff_b = grid[:, :, :, 1:] - grid[:, :, :, :-1]
    zero_pad = [(0, 0)] * 5
    after_a = list(zero_pad)
    after_a[2] = (0, 1)
    before_a = list(zero_pad)
    before_a[2] = (1, 0)
    after_b = list(zero_pad)
    after_b[3] = (0, 1)
    before_b = list(zero_pad)
    before_b[3] = (1, 0)
    return (
        jnp.pad(diff_a, after_a)
        - jnp.pad(diff_a, before_a)
        + jnp.pad(diff_b, after_b)
        - jnp.pad(diff_b, before_b)
    )


def on_device(x_start, data, u_fac, v_fac, ranks, slot_tile, neighbours):
    field_start = x_start[0]
    record = data[0, :, 0]
    ufac = u_fac[0, :, 0]
    vfac = v_fac[0, :, 0]
    rank_all = ranks[0, :, 0]
    slots = vfac.shape[1]
    count = ufac.shape[1]
    rows_own = record.shape[0]
    place = lax.axis_index("rtile")
    rank_tab = lax.dynamic_slice_in_dim(rank_all, place * rows_own, rows_own, 0)
    inverse = jnp.zeros((count,), jnp.int32).at[slot_tile].set(jnp.arange(count, dtype=jnp.int32))
    level = lax.broadcasted_iota(jnp.int32, rank_tab.shape + (RANK,), 2)
    kept_rows = (level < rank_tab[:, :, None]).astype(jnp.float32)[:, :, None, :, None]
    kept_half = kept_rows.astype(jnp.bfloat16)
    own_slots = place * slots + jnp.arange(slots, dtype=jnp.int32)
    own_tiles = slot_tile[own_slots]
    listed = neighbours[own_tiles]
    present = (listed >= 0).astype(jnp.float32)
    source_slot = inverse[jnp.maximum(listed, 0)]
    opposite = jnp.array([2, 3, 0, 1], dtype=jnp.int32)
    x_now = lax.all_gather(field_start, "stile", axis=3, tiled=True)
    z_now = x_now
    u_now = jnp.zeros_like(x_now)
    for step in range(ITERS):
        panel = conj_apply(vfac, x_now.astype(jnp.bfloat16), "iqrt,qtv->iqrv").astype(jnp.bfloat16)
        arrived = lax.all_to_all(panel, "rtile", split_axis=0, concat_axis=1, tiled=True)
        by_tile = jnp.take(arrived, inverse, axis=1) * kept_half
        image = plain_apply(ufac, by_tile, "sjrt,sjrv->stv")
        misfit = image - record
        back = conj_apply(ufac, misfit.astype(jnp.bfloat16), "sjrt,stv->sjrv")
        back = (back * kept_rows).astype(jnp.bfloat16)
        by_slot = jnp.take(back, slot_tile, axis=1)
        returned = lax.all_to_all(by_slot, "rtile", split_axis=1, concat_axis=0, tiled=True)
        partial_sum = plain_apply(vfac, returned, "iqrt,iqrv->qtv")
        grad_data = lax.psum(partial_sum, "stile")
        update_x_now = x_now
        update_z_now = z_now
        columns = update_x_now.shape[3]
        grid = update_x_now.reshape(slots, 2, EDGE, EDGE, columns)
        edges = jnp.stack(
            [
                grid[:, :, :, EDGE - 1, :],
                grid[:, :, EDGE - 1, :, :],
                grid[:, :, :, 0, :],
                grid[:, :, 0, :, :],
            ],
            axis=1,
        )
        every = lax.all_gather(edges, "rtile", axis=0, tiled=True)
        ghost = every[source_slot, opposite[None, :]] * present[:, :, None, None, None]
        lap = interior(grid)
        lap = lap.at[:, :, :, EDGE - 1, :].add(
            present[:, 0, None, None, None] * (ghost[:, 0] - grid[:, :, :, EDGE - 1, :])
        )
        lap = lap.at[:, :, EDGE - 1, :, :].add(
            present[:, 1, None, None, None] * (ghost[:, 1] - grid[:, :, EDGE - 1, :, :])
        )
        lap = lap.at[:, :, :, 0, :].add(
            present[:, 2, None, None, None] * (ghost[:, 2] - grid[:, :, :, 0, :])
        )
        lap = lap.at[:, :, 0, :, :].add(
            present[:, 3, None, None, None] * (ghost[:, 3] - grid[:, :, 0, :, :])
        )
        update_lap = lap.reshape(update_x_now.shape)
        update_x_now = update_x_now - 0.1 * (
            grad_data - 0.25 * update_lap + 1.0 * (update_x_now - update_z_now + u_now)
        )
        summed = update_x_now + u_now
        modulus = jnp.sqrt(summed[:, 0:1] ** 2 + summed[:, 1:2] ** 2)
        update_z_now = summed * (1.0 - 0.5 / jnp.maximum(modulus, 0.5))
        x_now = update_x_now
        z_now = update_z_now
        u_now = summed - update_z_now
    width = field_start.shape[3]
    offset = lax.axis_index("stile") * width
    x_now = lax.dynamic_slice_in_dim(x_now, offset, width, 3)
    z_now = lax.dynamic_slice_in_dim(z_now, offset, width, 3)
    return (x_now[None], z_now[None])


def solution(mesh):
    in_specs = (
        P(("band", "freq"), "rtile", None, None, "stile"),
        P(("band", "freq"), "rtile", "stile", None, None, None),
        P(("band", "freq"), "rtile", "stile", None, None, None, None),
        P(("band", "freq"), None, "stile", "rtile", None, None, None),
        P(("band", "freq"), None, "stile", None),
        P(),
        P(),
    )
    out_specs = (
        P(("band", "freq"), "rtile", None, None, "stile"),
        P(("band", "freq"), "rtile", None, None, "stile"),
    )
    return jax.shard_map(
        on_device, mesh=mesh, in_specs=in_specs, out_specs=out_specs, check_vma=False
    )
```

profile of v0, /device:TPU:0, one launch (start us, length us, event | category | flops | bytes accessed | tf_op | source)
XLA Modules:
  0.0 200.9 jit_solution(6304186878921996989)
XLA Ops:
  7.2 1.2 copy.426
  8.4 10.0 %all-gather = f32[1,2,2,256,128]{3,2,1,0,4:T(2,128)S(1)} all-gather(f32[1,2,2,256,64]{3,2,1,0,4:T(2,128)S(1)} %copy.426), channel_id=2, replica_groups=mesh['band'=2,'rtile'=4,'stile'=2,'freq'=2] {'stile'}, dimensions={4}, use_global_device_ids=true | all-gather | bytes 786432 | tf_op jit(solution)/shard_map/all_gather | solution.py:84
  19.7 0.7 copy.429
  20.5 5.1 %all-to-all-start = ((bf16[4,2,2,64,128]{4,3,1,2,0:T(8,128)(2,1)}), bf16[4,2,2,64,128]{4,3,1,2,0:T(8,128)(2,1)}, u32[]{:S(2)}, u32[]{:S(2)}) async-start(bf16[4,2,2,64,128]{4,3,1,2,0:T(8,128)(2,1)} %copy.429), calls=%async_computation | async-start | bytes 524288 | tf_op jit(solution)/shard_map/all_to_all | solution.py:89
  26.0 0.6 copy-done.1
  26.6 0.6 gather_fusion
  27.3 0.7 copy-done.39
  28.0 0.6 gather_fusion.1
  28.7 1.1 fusion.104
  29.8 0.8 slice_reduce_fusion
  30.6 0.6 scatter_custom_fusion
  31.3 0.5 compare_and_fusion
  31.8 0.6 pad_clamp_fusion.3
  32.6 15.3 %all_gather.10 = f32[8,4,2,16,128]{4,2,0,3,1:T(2,128)S(1)} all-gather(f32[2,4,2,16,128]{4,2,0,3,1:T(2,128)S(1)} %pad_maximum_fusion.4), channel_id=1, replica_groups=mesh['band'=2,'rtile'=4,'stile'=2,'freq'=2] {'rtile'}, dimensions={0}, use_global_device_ids=true | all-gather | bytes 655360 | tf_op jit(solution)/shard_map/all_gather | solution.py:112
  48.0 0.6 gather_fusion.2
  48.7 0.6 copy-done.40
  49.5 0.7 gather_fusion.3
  50.3 0.6 copy_subtract_fusion.4
  51.5 1.2 copy_subtract_fusion.5
  52.7 0.6 pad_clamp_fusion.4
  53.3 0.9 copy-done.23
  54.3 1.7 pad_subtract_fusion.1
  56.1 0.6 fusion.108
  56.7 1.0 copy.430
  57.7 0.7 gather_fusion.5
  58.4 0.6 copy-done.37
  61.2 0.7 gather_fusion.6
  61.9 0.6 copy-done.35
  62.5 0.8 fusion.54
  63.3 4.2 %all-to-all-start.1 = ((bf16[1,8,2,64,128]{4,3,2,0,1:T(8,128)(2,1)}), bf16[1,8,2,64,128]{4,3,2,0,1:T(8,128)(2,1)}, u32[]{:S(2)}, u32[]{:S(2)}) async-start(bf16[1,8,2,64,128]{4,3,2,0,1:T(8,128)(2,1)} %fusion.54), calls=%async_computation.1 | async-start | bytes 524288 | tf_op jit(solution)/shard_map/all_to_all | solution.py:96
  67.6 0.6 copy-done.33
  68.4 0.7 copy-done.24
  69.1 0.7 copy-done.10
  70.1 4.2 %all-to-all-done.1 = bf16[1,8,2,64,128]{4,3,2,0,1:T(8,128)(2,1)} async-done(((bf16[1,8,2,64,128]{4,3,2,0,1:T(8,128)(2,1)}), bf16[1,8,2,64,128]{4,3,2,0,1:T(8,128)(2,1)}, u32[]{:S(2)}, u32[]{:S(2)}) %all-to-all-start.1) | async-done | bytes 262176 | tf_op jit(solution)/shard_map/all_to_all | solution.py:96
  74.3 1.0 fusion.107
  76.5 0.9 pad_maximum_fusion
  77.4 0.7 copy-done.20
  78.5 0.6 slice.572
  79.1 0.6 copy-done.27
  79.8 0.8 fusion.77
  80.6 25.3 %all-reduce.11.cloned.1.call-done = f32[2,2,256,128]{3,2,0,1:T(8,128)} async-done(((f32[2,2,256,128]{3,2,0,1:T(8,128)}), f32[2,2,256,128]{3,2,0,1:T(8,128)}) %all-reduce.11.cloned.1.call-update) | async-done | bytes 524304 | tf_op jit(solution)/shard_map/psum | solution.py:98
  105.9 1.2 fusion.97
  107.2 1.1 fusion.100
  108.4 0.9 fusion.58
  109.9 16.2 %all_gather.11 = f32[8,4,2,16,128]{4,3,2,1,0:T(8,128)} all-gather(f32[2,4,2,16,128]{4,3,2,1,0:T(8,128)S(1)} %copy.491), channel_id=1, replica_groups=mesh['band'=2,'rtile'=4,'stile'=2,'freq'=2] {'rtile'}, dimensions={0}, use_global_device_ids=true | all-gather | bytes 655360 | tf_op jit(solution)/shard_map/all_gather | solution.py:112
  126.0 1.6 gather_fusion.4
  127.6 0.8 copy_multiply_fusion
  128.4 1.9 copy_subtract_fusion.3
  130.3 0.6 copy_subtract_fusion.2
  132.7 0.7 copy.468
  133.4 5.6 %all-to-all-start.2 = ((bf16[4,2,2,64,128]{4,3,1,2,0:T(8,128)(2,1)}), bf16[4,2,2,64,128]{4,3,1,2,0:T(8,128)(2,1)S(1)}, u32[]{:S(2)}, u32[]{:S(2)}) async-start(bf16[4,2,2,64,128]{4,3,1,2,0:T(8,128)(2,1)} %copy.468), calls=%async_computation.2 | async-start | bytes 524288 | tf_op jit(solution)/shard_map/all_to_all | solution.py:89
  139.4 0.7 copy-done.16
  140.3 5.6 %all-to-all-done.2 = bf16[4,2,2,64,128]{4,3,1,2,0:T(8,128)(2,1)S(1)} async-done(((bf16[4,2,2,64,128]{4,3,1,2,0:T(8,128)(2,1)}), bf16[4,2,2,64,128]{4,3,1,2,0:T(8,128)(2,1)S(1)}, u32[]{:S(2)}, u32[]{:S(2)}) %all-to-all-start.2) | async-done | bytes 262176 | tf_op jit(solution)/shard_map/all_to_all | solution.py:89
  145.9 0.7 gather_fusion.7
  148.8 0.7 gather_fusion.8
  149.6 0.8 fusion.52
  150.4 3.6 %all-to-all-start.3 = ((bf16[1,8,2,64,128]{4,3,2,0,1:T(8,128)(2,1)}), bf16[1,8,2,64,128]{4,3,2,0,1:T(8,128)(2,1)S(1)}, u32[]{:S(2)}, u32[]{:S(2)}) async-start(bf16[1,8,2,64,128]{4,3,2,0,1:T(8,128)(2,1)} %fusion.52), calls=%async_computation.3 | async-start | bytes 524288 | tf_op jit(solution)/shard_map/all_to_all | solution.py:96
  154.3 0.7 copy-done.12
  155.1 5.6 %all-to-all-done.3 = bf16[1,8,2,64,128]{4,3,2,0,1:T(8,128)(2,1)S(1)} async-done(((bf16[1,8,2,64,128]{4,3,2,0,1:T(8,128)(2,1)}), bf16[1,8,2,64,128]{4,3,2,0,1:T(8,128)(2,1)S(1)}, u32[]{:S(2)}, u32[]{:S(2)}) %all-to-all-start.3) | async-done | bytes 262176 | tf_op jit(solution)/shard_map/all_to_all | solution.py:96
  161.8 0.9 pad_maximum_fusion.1
  162.9 27.4 %all-reduce.13.cloned.1.call-done = f32[2,2,256,128]{3,2,0,1:T(8,128)} async-done(((f32[2,2,256,128]{3,2,0,1:T(8,128)}), f32[2,2,256,128]{3,2,0,1:T(8,128)}) %all-reduce.13.cloned.1.call-update) | async-done | bytes 524304 | tf_op jit(solution)/shard_map/psum | solution.py:98
  190.4 1.2 fusion.35
  192.1 0.9 copy.504
  193.2 0.9 copy.503
  (185 shorter events, 14.7 us)
Async XLA Ops:
  7.2 42.2 %copy-start = (s32[1,4,1,8]{3,2,1,0:T(1,128)S(1)}, s32[1,4,1,8]{3,2,1,0:T(1,128)}, u32[]{:S(2)}) copy-start(s32[1,4,1,8]{3,2,1,0:T(1,128)} %param.30) | copy-start | bytes 388
  8.3 10.1 %copy-start.5 = (bf16[1,4,1,2,2,64,256]{6,5,4,3,2,1,0:T(8,128)(2,1)S(1)}, bf16[1,4,1,2,2,64,256]{6,5,4,3,2,1,0:T(8,128)(2,1)}, u32[]{:S(2)}) copy-start(bf16[1,4,1,2,2,64,256]{6,5,4,3,2,1,0:T(8,128)(2,1)} %param.29) | copy-start | bytes 1572868
  20.5 36.2 %all-to-all-start = ((bf16[4,2,2,64,128]{4,3,1,2,0:T(8,128)(2,1)}), bf16[4,2,2,64,128]{4,3,1,2,0:T(8,128)(2,1)}, u32[]{:S(2)}, u32[]{:S(2)}) async-start(bf16[4,2,2,64,128]{4,3,1,2,0:T(8,128)(2,1)} %copy.429), calls=%async_computation | async-start | bytes 524288 | tf_op jit(solution)/shard_map/all_to_all | solution.py:89
  25.9 6.6 %copy-start.19 = (f32[2,2,16,1,128]{4,3,2,1,0:T(1,128)}, f32[2,2,16,1,128]{4,3,2,1,0:T(1,128)S(1)}, u32[]{:S(2)}) copy-start(f32[2,2,16,1,128]{4,3,2,1,0:T(1,128)S(1)} %get-tuple-element.116) | copy-start | bytes 98308
  25.9 6.6 %copy-start.21 = (f32[2,2,16,1,128]{4,3,2,1,0:T(1,128)}, f32[2,2,16,1,128]{4,3,2,1,0:T(1,128)S(1)}, u32[]{:S(2)}) copy-start(f32[2,2,16,1,128]{4,3,2,1,0:T(1,128)S(1)} %get-tuple-element.115) | copy-start | bytes 98308
  25.9 6.5 %copy-start.9 = (f32[2,2,1,16,128]{4,3,2,1,0:T(8,128)}, f32[2,2,1,16,128]{4,3,2,1,0:T(8,128)S(1)}, u32[]{:S(2)}) copy-start(f32[2,2,1,16,128]{4,3,2,1,0:T(8,128)S(1)} %get-tuple-element.117) | copy-start | bytes 98308
  26.0 0.7 copy-start.1
  27.3 0.7 copy-start.39
  29.8 20.4 %copy-start.26 = (f32[2,4]{0,1:T(4,128)}, f32[2,4]{0,1:T(4,128)S(1)}, u32[]{:S(2)}) copy-start(f32[2,4]{0,1:T(4,128)S(1)} %copy.572) | copy-start | bytes 100
  48.6 0.7 copy-start.40
  50.3 1.0 copy-start.2
  50.3 1.2 copy-start.3
  51.5 1.8 copy-start.6
  53.3 1.0 copy-start.23
  58.4 0.6 copy-start.37
  61.9 0.6 copy-start.35
  63.3 4.3 %copy-start.22 = (f32[2,2,16,1,128]{4,3,2,1,0:T(1,128)S(1)}, f32[2,2,16,1,128]{4,3,2,1,0:T(1,128)}, u32[]{:S(2)}) copy-start(f32[2,2,16,1,128]{4,3,2,1,0:T(1,128)} %copy-done.21) | copy-start | bytes 98308
  63.3 4.3 %copy-start.25 = (f32[2,1,2,16,128]{4,3,2,0,1:T(8,128)S(1)}, f32[2,1,2,16,128]{4,3,2,0,1:T(8,128)}, u32[]{:S(2)}) copy-start(f32[2,1,2,16,128]{4,3,2,0,1:T(8,128)} %get-tuple-element.128) | copy-start | bytes 98308
  63.3 11.0 %all-to-all-start.1 = ((bf16[1,8,2,64,128]{4,3,2,0,1:T(8,128)(2,1)}), bf16[1,8,2,64,128]{4,3,2,0,1:T(8,128)(2,1)}, u32[]{:S(2)}, u32[]{:S(2)}) async-start(bf16[1,8,2,64,128]{4,3,2,0,1:T(8,128)(2,1)} %fusion.54), calls=%async_computation.1 | async-start | bytes 524288 | tf_op jit(solution)/shard_map/all_to_all | solution.py:96
  67.5 38.4 %all-reduce.11.cloned.1.call-start = ((), (), s32[]{:S(2)}) async-start(), calls=%async_computation.4 | async-start | bytes 1048576 | tf_op jit(solution)/shard_map/psum | solution.py:98
  67.6 0.7 copy-start.33
  68.3 0.8 copy-start.24
  69.1 0.8 copy-start.10
  69.1 0.7 copy-start.31
  77.3 0.8 copy-start.20
  77.4 0.7 copy-start.29
  79.1 0.6 copy-start.27
  107.1 2.4 %copy-start.15 = (f32[2,2,1,16,128]{4,3,2,0,1:T(8,128)}, f32[2,2,1,16,128]{4,3,2,0,1:T(8,128)S(1)}, u32[]{:S(2)}) copy-start(f32[2,2,1,16,128]{4,3,2,0,1:T(8,128)S(1)} %get-tuple-element.109) | copy-start | bytes 98308
  107.1 2.5 %copy-start.11 = (f32[2,2,1,16,128]{4,3,2,0,1:T(8,128)}, f32[2,2,1,16,128]{4,3,2,0,1:T(8,128)S(1)}, u32[]{:S(2)}) copy-start(f32[2,2,1,16,128]{4,3,2,0,1:T(8,128)S(1)} %get-tuple-element.110) | copy-start | bytes 98308
  107.2 2.5 %copy-start.13 = (f32[2,2,16,1,128]{4,3,2,0,1:T(1,128)}, f32[2,2,16,1,128]{4,3,2,0,1:T(1,128)S(1)}, u32[]{:S(2)}) copy-start(f32[2,2,16,1,128]{4,3,2,0,1:T(1,128)S(1)} %get-tuple-element.108) | copy-start | bytes 98308
  107.2 2.5 %copy-start.17 = (f32[2,2,16,1,128]{4,3,2,0,1:T(1,128)}, f32[2,2,16,1,128]{4,3,2,0,1:T(1,128)S(1)}, u32[]{:S(2)}) copy-start(f32[2,2,16,1,128]{4,3,2,0,1:T(1,128)S(1)} %get-tuple-element.107) | copy-start | bytes 98308
  128.4 3.2 %copy-start.7 = (f32[2,4,2,16,128]{4,2,0,3,1:T(2,128)}, f32[2,4,2,16,128]{4,2,0,3,1:T(2,128)S(1)}, u32[]{:S(2)}) copy-start(f32[2,4,2,16,128]{4,2,0,3,1:T(2,128)S(1)} %copy_multiply_fusion) | copy-start | bytes 393220
  131.2 0.8 copy-start.18
  131.2 0.8 copy-start.34
  131.2 1.0 copy-start.4
  133.4 6.0 %copy-start.8 = (f32[2,4,2,16,128]{4,2,0,3,1:T(2,128)S(1)}, f32[2,4,2,16,128]{4,2,0,3,1:T(2,128)}, u32[]{:S(2)}) copy-start(f32[2,4,2,16,128]{4,2,0,3,1:T(2,128)} %copy-done.7) | copy-start | bytes 393220
  133.4 12.4 %all-to-all-start.2 = ((bf16[4,2,2,64,128]{4,3,1,2,0:T(8,128)(2,1)}), bf16[4,2,2,64,128]{4,3,1,2,0:T(8,128)(2,1)S(1)}, u32[]{:S(2)}, u32[]{:S(2)}) async-start(bf16[4,2,2,64,128]{4,3,1,2,0:T(8,128)(2,1)} %copy.468), calls=%async_computation.2 | async-start | bytes 524288 | tf_op jit(solution)/shard_map/all_to_all | solution.py:89
  139.4 0.8 copy-start.16
  139.4 0.8 copy-start.32
  145.9 0.7 copy-start.38
  148.8 0.7 copy-start.36
  150.4 3.6 %copy-start.14 = (f32[2,2,16,1,128]{4,3,2,0,1:T(1,128)S(1)}, f32[2,2,16,1,128]{4,3,2,0,1:T(1,128)}, u32[]{:S(2)}) copy-start(f32[2,2,16,1,128]{4,3,2,0,1:T(1,128)} %copy-done.13) | copy-start | bytes 98308
  150.4 3.6 %copy-start.30 = (f32[2]{0:T(128)S(1)}, f32[2]{0:T(128)}, u32[]{:S(2)}) copy-start(f32[2]{0:T(128)} %get-tuple-element.100) | copy-start | bytes 28
  150.4 10.3 %all-to-all-start.3 = ((bf16[1,8,2,64,128]{4,3,2,0,1:T(8,128)(2,1)}), bf16[1,8,2,64,128]{4,3,2,0,1:T(8,128)(2,1)S(1)}, u32[]{:S(2)}, u32[]{:S(2)}) async-start(bf16[1,8,2,64,128]{4,3,2,0,1:T(8,128)(2,1)} %fusion.52), calls=%async_computation.3 | async-start | bytes 524288 | tf_op jit(solution)/shard_map/all_to_all | solution.py:96
  153.9 36.4 %all-reduce.13.cloned.1.call-start = ((), (), s32[]{:S(2)}) async-start(), calls=%async_computation.5 | async-start | bytes 1048576 | tf_op jit(solution)/shard_map/psum | solution.py:98
  154.3 0.8 copy-start.12
  154.3 0.8 copy-start.28
Sparse Core Ops, SparseCore 0:
  77.5 28.4 all-reduce.10
  162.8 27.4 all-reduce.12
where the time goes:
time: 202 us; the launch traced here: 201 us
  waiting for transfers between devices  68.2 us (34%)
  blocking collectives  41.5 us (21%)
  local copies, waits for them, and re-layouts  31.6 us (16%)
  starting transfers between devices  18.6 us (9%)
  other arithmetic  17.6 us (9%)
  between operations  15.1 us (7%)
  matrix products  8.43 us (4%)
    psum x2, waiting for transfers between devices, on_device(): grad_data = lax.psum(partial_sum, 'stile')  52.7 us
    all_gather x2, blocking collectives, on_device(): every = lax.all_gather(edges, 'rtile', axis=0, tiled=True)  31.5 us
    unnamed x94, local copies, waits for them, and re-layouts  11.7 us
    all_to_all x2, starting transfers between devices, on_device(): lax.all_to_all(panel, 'rtile', split_axis=0, concat_axis=1, tiled=True)  10.7 us
    all_gather x1, blocking collectives, on_device(): x_now = lax.all_gather(field_start, 'stile', axis=3, tiled=True)  10 us
    all_to_all x2, waiting for transfers between devices, on_device(): lax.all_to_all(by_slot, 'rtile', split_axis=1, concat_axis=0, tiled=True)  9.8 us
    all_to_all x2, starting transfers between devices, on_device(): lax.all_to_all(by_slot, 'rtile', split_axis=1, concat_axis=0, tiled=True)  7.74 us
    all_to_all x2, waiting for transfers between devices, on_device(): lax.all_to_all(panel, 'rtile', split_axis=0, concat_axis=1, tiled=True)  5.58 us
  transfers between devices with their start and end apart: 6, of which 5 were waited for; matrix products, arithmetic and copies ran while one was open for 8% of the time, Pallas kernels for 0%

commit v1 on v0

v1 whole, which is shorter than its diff:
```python
import functools

import jax
import jax.numpy as jnp
from jax import lax
from jax.experimental import pallas as pl
from jax.experimental.pallas import tpu as pltpu
from jax.sharding import PartitionSpec as P

EDGE = 16
ITERS = 2
F32 = jnp.float32
BF16 = jnp.bfloat16
MESH = pl.DeviceIdType.MESH


def dot(a, b):
    return lax.dot_general(a, b, (((1,), (0,)), ((), ())), preferred_element_type=F32)


def dot_t(a, b):
    return lax.dot_general(a, b, (((0,), (0,)), ((), ())), preferred_element_type=F32)


def swap(v):
    w = v.shape[1] // 2
    if v.shape[1] == 128:
        return pltpu.roll(v, w, 1)
    return jnp.concatenate([v[:, w:], v[:, :w]], axis=1)


def shift(v, by):
    n = v.shape[0]
    return pltpu.roll(v, by % n, 0)


def kernel(
    R, S,
    x_ref, d_ref, u_ref, v_ref, rk_ref, st_ref, nb_ref,
    xo_ref, zo_ref,
    vp, mk, up, dl, xs, zs, us,
    pan_out, pan_in, back_out, back_in, edge_out, edge_in0, edge_in1,
    v_send, v_recv, m_send, m_recv, p_send, p_recv, b_send, b_recv, e_send, e_recv,
):
    me_i = lax.axis_index("rtile")
    me_c = lax.axis_index("stile")
    rank = v_ref.shape[-2]
    tile = v_ref.shape[-1]
    w = x_ref.shape[-1]
    w2 = 2 * w
    count = st_ref.shape[0]
    blk = rank // 8

    barrier = pltpu.get_barrier_semaphore()
    for d in range(S):
        for k in range(R):
            if d or k:
                pl.semaphore_signal(
                    barrier, inc=1,
                    device_id={"rtile": lax.rem(me_i + k, R), "stile": lax.rem(me_c + d, S)},
                    device_id_type=MESH,
                )

    row = lax.broadcasted_iota(jnp.int32, (rank, tile), 0)

    def packed(a, b, ra, rb):
        a = a.astype(F32)
        b = b.astype(F32)
        b = jnp.concatenate([b[j * blk:(j + 1) * blk] for j in reversed(range(8))], axis=0)
        return jnp.where(row < ra, a, jnp.where(row >= rank - rb, b, 0.0)).astype(BF16)

    level = lax.broadcasted_iota(jnp.int32, (8, w2), 0) * blk
    own_a = st_ref[2 * me_i]
    own_b = st_ref[2 * me_i + 1]
    for i in range(R):
        ra = rk_ref[0, i, 0, own_a]
        rb = rk_ref[0, i, 0, own_b]
        for c in range(2):
            vp[0, c, i * rank:(i + 1) * rank, :] = packed(
                v_ref[0, i, 0, 0, c], v_ref[0, i, 0, 1, c], ra, rb
            )
        mk[0, i * 8:(i + 1) * 8, :] = (level < ra).astype(F32)

    pl.semaphore_wait(barrier, R * S - 1)

    pending = []

    def send(src, dst, ss, rs, i, c):
        copy = pltpu.make_async_remote_copy(
            src_ref=src, dst_ref=dst, send_sem=ss, recv_sem=rs,
            device_id={"rtile": i, "stile": c}, device_id_type=MESH,
        )
        copy.start()
        pending.append(copy)
        return copy

    v_copies = {}
    for d in range(1, S):
        c = lax.rem(me_c + S - d, S)
        v_copies[d] = (
            send(vp.at[0], vp.at[d], v_send.at[d], v_recv.at[d], me_i, c),
            send(mk.at[0], mk.at[d], m_send.at[d], m_recv.at[d], me_i, c),
        )

    for q in range(2):
        xs[q] = jnp.concatenate([x_ref[0, q, 0], x_ref[0, q, 1]], axis=1)

    lane = lax.broadcasted_iota(jnp.int32, (1, w2), 1)
    sgn = jnp.where(lane < w, 1.0, -1.0).astype(F32)

    cell = lax.broadcasted_iota(jnp.int32, (tile, w2), 0)
    ca = cell // EDGE
    cb = cell % EDGE
    has_e = (cb < EDGE - 1).astype(F32)
    has_w = (cb > 0).astype(F32)
    has_s = (ca < EDGE - 1).astype(F32)
    has_n = (ca > 0).astype(F32)

    def one_hot(shape, edge_dim):
        e = lax.broadcasted_iota(jnp.int32, shape, edge_dim)
        at = lax.broadcasted_iota(jnp.int32, shape, 1 - edge_dim)
        side = e // EDGE
        j = e % EDGE
        want = jnp.where(
            side == 0, j * EDGE + EDGE - 1,
            jnp.where(side == 1, (EDGE - 1) * EDGE + j, jnp.where(side == 2, j * EDGE, j)),
        )
        return (at == want).astype(F32).astype(BF16)

    take_edges = one_hot((4 * EDGE, tile), 0)
    put_edges = one_hot((tile, 4 * EDGE), 1)

    def mask_of(d):
        m = mk[d]
        return jnp.broadcast_to(m[:, None, :], (R * 8, blk, w2)).reshape(R * rank, w2) > 0.5

    for t in range(ITERS):
        edge_in = (edge_in0, edge_in1)[t]
        x0 = xs[0]
        x1 = xs[1]
        rhs_r = jnp.concatenate([x0, x1], axis=1).astype(BF16)
        rhs_i = jnp.concatenate([swap(x0) * sgn, swap(x1) * sgn], axis=1).astype(BF16)

        p_copies = []
        for d in range(S):
            if t == 0 and d:
                for copy in v_copies[d]:
                    copy.wait_recv()
            both = dot(vp[d, 0], rhs_r) + dot(vp[d, 1], rhs_i)
            pan = jnp.where(mask_of(d), both[:, :w2], both[:, w2:]).astype(BF16)
            pan_out[t, d] = pan.reshape(R, rank, w2)
            for k in reversed(range(R)):
                if d or k:
                    i = lax.rem(me_i + k, R)
                    p_copies.append(send(
                        pan_out.at[t, d, i], pan_in.at[t, d, me_i],
                        p_send.at[t, d, k], p_recv.at[t, d, k],
                        i, lax.rem(me_c + d, S),
                    ))
        pan_in[t, 0, me_i] = pan_out[t, 0, me_i]

        edges = dot(take_edges, rhs_r).astype(BF16)
        for q in range(2):
            edge_out[t, q] = edges[:, q * w2:(q + 1) * w2]
            edge_in[2 * me_i + q] = edges[:, q * w2:(q + 1) * w2]
        e_copies = []
        for k in range(1, R):
            e_copies.append(send(
                edge_out.at[t], edge_in.at[pl.ds(2 * me_i, 2)],
                e_send.at[t, k], e_recv.at[t, k], lax.rem(me_i + k, R), me_c,
            ))

        if t == 0:
            for p in range(R):
                ta = st_ref[2 * p]
                tb = st_ref[2 * p + 1]
                ra = rk_ref[0, me_i, 0, ta]
                rb = rk_ref[0, me_i, 0, tb]
                for c in range(2):
                    up[c, p * rank:(p + 1) * rank, :] = packed(
                        u_ref[0, 0, 0, ta, c], u_ref[0, 0, 0, tb, c], ra, rb
                    )
            for s in range(S):
                dl[s] = jnp.concatenate(
                    [d_ref[0, 0, 0, 0, :, s * w:(s + 1) * w], d_ref[0, 0, 0, 1, :, s * w:(s + 1) * w]],
                    axis=1,
                )

        for copy in p_copies:
            copy.wait_recv()
        b_copies = []
        for e in range(S):
            pan = pan_in[t, e].reshape(R * rank, w2)
            turned = (swap(pan.astype(F32)) * (-sgn)).astype(BF16)
            image = dot_t(up[0], pan) + dot_t(up[1], turned)
            misfit = image - dl[lax.rem(me_c + S - e, S)]
            mis_r = misfit.astype(BF16)
            mis_i = (swap(misfit) * sgn).astype(BF16)
            back = (dot(up[0], mis_r) + dot(up[1], mis_i)).astype(BF16)
            back_out[t, e] = back.reshape(R, rank, w2)
            for k in reversed(range(R)):
                if e or k:
                    q = lax.rem(me_i + k, R)
                    b_copies.append(send(
                        back_out.at[t, e, q], back_in.at[t, e, me_i],
                        b_send.at[t, e, k], b_recv.at[t, e, k],
                        q, lax.rem(me_c + S - e, S),
                    ))
        back_in[t, 0, me_i] = back_out[t, 0, me_i]

        for copy in e_copies:
            copy.wait_recv()
        ghosts = []
        degs = []
        for q in range(2):
            mine = st_ref[2 * me_i + q]
            parts = []
            deg = has_e + has_w + has_s + has_n
            for side in range(4):
                listed = nb_ref[mine, side]
                present = jnp.where(listed >= 0, 1.0, 0.0).astype(F32)
                want = jnp.maximum(listed, 0)
                slot = jnp.int32(0)
                for j in range(count):
                    slot = jnp.where(st_ref[j] == want, j, slot)
                opp = (side + 2) % 4
                ghost = edge_in[slot, opp * EDGE:(opp + 1) * EDGE, :].astype(F32)
                parts.append(ghost * present)
                border = (has_e, has_s, has_w, has_n)[side]
                deg = deg + (1.0 - border) * present
            ghosts.append(jnp.concatenate(parts, axis=0))
            degs.append(deg)
        ghost_sum = dot(put_edges, jnp.concatenate(ghosts, axis=1).astype(BF16))
        drift = []
        for q in range(2):
            x = xs[q]
            lap = (
                shift(x, -1) * has_e + shift(x, 1) * has_w
                + shift(x, -EDGE) * has_s + shift(x, EDGE) * has_n
                + ghost_sum[:, q * w2:(q + 1) * w2] - degs[q] * x
            )
            term = -0.25 * lap
            if t:
                term = term + (x - zs[q] + us[q])
            drift.append(term)

        for copy in b_copies:
            copy.wait_recv()
        grad = jnp.zeros((tile, 2 * w2), F32)
        for d in range(S):
            b = back_in[t, d].reshape(R * rank, w2).astype(F32)
            turned = swap(b) * (-sgn)
            m = mask_of(d)
            g_r = jnp.concatenate([jnp.where(m, b, 0.0), jnp.where(m, 0.0, b)], axis=1).astype(BF16)
            g_i = jnp.concatenate([jnp.where(m, turned, 0.0), jnp.where(m, 0.0, turned)], axis=1).astype(BF16)
            grad = grad + dot_t(vp[d, 0], g_r) + dot_t(vp[d, 1], g_i)

        for q in range(2):
            x = xs[q] - 0.1 * (grad[:, q * w2:(q + 1) * w2] + drift[q])
            summed = x + us[q] if t else x
            sq = summed * summed
            modulus = jnp.sqrt(sq + swap(sq))
            z = summed * (1.0 - 0.5 / jnp.maximum(modulus, 0.5))
            if t < ITERS - 1:
                xs[q] = x
                zs[q] = z
                us[q] = summed - z
            else:
                for c in range(2):
                    xo_ref[0, q, c] = x[:, c * w:(c + 1) * w]
                    zo_ref[0, q, c] = z[:, c * w:(c + 1) * w]

    for copy in pending:
        copy.wait_send()


def on_device(R, S, x_start, data, u_fac, v_fac, ranks, slot_tile, neighbours):
    w2 = 2 * x_start.shape[-1]
    tile = x_start.shape[-2]
    rank = v_fac.shape[-2]
    slots = x_start.shape[1]
    T = ITERS
    vmem = pl.BlockSpec(memory_space=pltpu.VMEM)
    smem = pl.BlockSpec(memory_space=pltpu.SMEM)
    out = jax.ShapeDtypeStruct(x_start.shape, F32)
    dma = pltpu.SemaphoreType.DMA
    return pl.pallas_call(
        functools.partial(kernel, R, S),
        out_shape=(out, out),
        in_specs=[vmem, vmem, vmem, vmem, smem, smem, smem],
        out_specs=(vmem, vmem),
        scratch_shapes=[
            pltpu.VMEM((S, 2, R * rank, tile), BF16),
            pltpu.VMEM((S, R * 8, w2), F32),
            pltpu.VMEM((2, R * rank, tile), BF16),
            pltpu.VMEM((S, tile, w2), F32),
            pltpu.VMEM((slots, tile, w2), F32),
            pltpu.VMEM((slots, tile, w2), F32),
            pltpu.VMEM((slots, tile, w2), F32),
            pltpu.VMEM((T, S, R, rank, w2), BF16),
            pltpu.VMEM((T, S, R, rank, w2), BF16),
            pltpu.VMEM((T, S, R, rank, w2), BF16),
            pltpu.VMEM((T, S, R, rank, w2), BF16),
            pltpu.VMEM((T, slots, 4 * EDGE, w2), BF16),
            pltpu.VMEM((slots * R, 4 * EDGE, w2), BF16),
            pltpu.VMEM((slots * R, 4 * EDGE, w2), BF16),
            dma((S,)), dma((S,)), dma((S,)), dma((S,)),
            dma((T, S, R)), dma((T, S, R)), dma((T, S, R)), dma((T, S, R)),
            dma((T, R)), dma((T, R)),
        ],
        compiler_params=pltpu.CompilerParams(
            collective_id=0, has_side_effects=True, vmem_limit_bytes=56 * 1024 * 1024
        ),
    )(x_start, data, u_fac, v_fac, ranks, slot_tile, neighbours)


def solution(mesh):
    in_specs = (
        P(("band", "freq"), "rtile", None, None, "stile"),
        P(("band", "freq"), "rtile", "stile", None, None, None),
        P(("band", "freq"), "rtile", "stile", None, None, None, None),
        P(("band", "freq"), None, "stile", "rtile", None, None, None),
        P(("band", "freq"), None, "stile", None),
        P(),
        P(),
    )
    out_specs = (
        P(("band", "freq"), "rtile", None, None, "stile"),
        P(("band", "freq"), "rtile", None, None, "stile"),
    )
    return jax.shard_map(
        functools.partial(on_device, mesh.shape["rtile"], mesh.shape["stile"]),
        mesh=mesh, in_specs=in_specs, out_specs=out_specs, check_vma=False,
    )
```

time: 202 us -> 44.9 us (0.22)
  waiting for transfers between devices: 68.2 us -> 0 us
  blocking collectives: 41.5 us -> 0 us
  Pallas kernels: 0 us -> 37.8 us
  local copies, waits for them, and re-layouts: 31.6 us -> 6.16 us
  starting transfers between devices: 18.6 us -> 0 us
  other arithmetic: 17.6 us -> 0 us
  between operations: 15.1 us -> 0.65 us
  matrix products: 8.43 us -> 0 us
    psum x2 -> x0, waiting for transfers between devices: 52.7 us -> none  [on_device(): grad_data = lax.psum(partial_sum, 'stile')]
    all_gather x3 -> x0, blocking collectives: 41.5 us -> none  [the longest x2 31.5 us: on_device(): every = lax.all_gather(edges, 'rtile', axis=0, tiled=True)]
    pallas_call x0 -> x1, Pallas kernels: none -> 37.8 us  [on_device(): pl.pallas_call(functools.partial(kernel, R, S), out_shape=(out, out), in_...]
    all_to_all x4 -> x0, starting transfers between devices: 18.5 us -> none  [the longest x2 10.7 us: on_device(): lax.all_to_all(panel, 'rtile', split_axis=0, concat_axis=1, tiled=True)]
    all_to_all x4 -> x0, waiting for transfers between devices: 15.4 us -> none  [the longest x2 9.8 us: on_device(): lax.all_to_all(by_slot, 'rtile', split_axis=1, concat_axis=0, tiled=True)]
    dot_general x32 -> x0, matrix products: 8.43 us -> none  [the longest x4 1.6 us: conj_apply(): jnp.einsum(form, factor[..., 0, :, :], field[..., 0, :, :], preferred_ele...]
    unnamed x94 -> x4, local copies, waits for them, and re-layouts: 11.7 us -> 3.29 us
    gather x10 -> x0, local copies, waits for them, and re-layouts: 7.12 us -> none  [the longest x2 2.33 us: on_device(): every[source_slot, opposite[None, :]] * present[:, :, None, None, None]]
  transfers between devices with their start and end apart: 6 -> 0, of which waited for: 5 -> 0; matrix products, arithmetic and copies ran while one was open for 8% -> 0% of each run, Pallas kernels for 0% -> 0%
where the time goes in v1:
time: 44.9 us; the launch traced here: 44.7 us
  Pallas kernels  37.8 us (84%)
  local copies, waits for them, and re-layouts  6.16 us (14%)
  between operations  0.65 us (1%)
    pallas_call x1, Pallas kernels, on_device(): pl.pallas_call(functools.partial(kernel, R, S), out_shape=(out, out), in_...  37.8 us
    unnamed x4, local copies, waits for them, and re-layouts  3.29 us
    pallas_call x2, local copies, waits for them, and re-layouts, on_device(): pl.pallas_call(functools.partial(kernel, R, S), out_shape=(out, out), in_...  2.87 us

profile of v1, /device:TPU:0, one launch (start us, length us, event | category | flops | bytes accessed | tf_op | source)
XLA Modules:
  0.0 44.7 jit_solution(232874019309225257)
XLA Ops:
  0.6 1.3 %copy.10.nb_ref = s32[8,4]{1,0:T(8,128)} copy(s32[8,4]{0,1:T(4,128)} %param.13) | data formatting | bytes 256 | tf_op args[6]
  2.0 1.9 %copy.9.x_ref = f32[1,2,2,256,64]{4,3,2,1,0:T(8,128)} copy(f32[1,2,2,256,64]{3,4,2,1,0:T(8,128)} %param.7) | data formatting | bytes 524288 | tf_op args[0]
  3.9 37.8 %shard_map.86 = (f32[1,2,2,256,64]{4,3,2,1,0:T(8,128)}, f32[1,2,2,256,64]{4,3,2,1,0:T(8,128)}) custom-call(f32[1,2,2,256,64]{4,3,2,1,0:T(8,128)} %copy.9.x_ref, f32[1,1,1,2,256,128]{5,4,3,2,1,0:T(8,128)} %d_ref.1, bf16[1,1,1,8,2,64,256]{6,5,4,3,2,1,0:T(8,128)(2,1)} %u_ref.1, bf16[1,4,1,2,2,64,256]{6,5,4,3,2,1,0:T(8,128)(2,1)} %v_ref.1, ...), custom_call_target="tpu_custom_call" | custom-call | tf_op jit(solution)/shard_map/pallas_call | solution.py:287
  41.8 0.0 copy-start
  41.8 2.0 %copy.11 = f32[1,2,2,256,64]{3,4,2,1,0:T(8,128)} copy(f32[1,2,2,256,64]{4,3,2,1,0:T(8,128)} %get-tuple-element.2) | data formatting | bytes 524288 | tf_op jit(solution)/shard_map/pallas_call | solution.py:287
  43.8 0.0 copy-done
  43.8 0.9 %copy.12 = f32[1,2,2,256,64]{3,4,2,1,0:T(8,128)} copy(f32[1,2,2,256,64]{4,3,2,1,0:T(8,128)S(1)} %copy-done) | data formatting | bytes 524288 | tf_op jit(solution)/shard_map/pallas_call | solution.py:287
Async XLA Ops:
  41.8 2.0 %copy-start = (f32[1,2,2,256,64]{4,3,2,1,0:T(8,128)S(1)}, f32[1,2,2,256,64]{4,3,2,1,0:T(8,128)}, u32[]{:S(2)}) copy-start(f32[1,2,2,256,64]{4,3,2,1,0:T(8,128)} %get-tuple-element.3) | copy-start | bytes 786436

commit v2 on v1

--- a/solution.py
+++ b/solution.py
@@ -38,15 +38,15 @@
     R, S,
     x_ref, d_ref, u_ref, v_ref, rk_ref, st_ref, nb_ref,
     xo_ref, zo_ref,
-    vp, mk, up, dl, xs, zs, us,
+    xv, dv, uv, vv, vp, mk, up, dl, xs, zs, us, xb,
     pan_out, pan_in, back_out, back_in, edge_out, edge_in0, edge_in1,
-    v_send, v_recv, m_send, m_recv, p_send, p_recv, b_send, b_recv, e_send, e_recv,
+    in_sem, x_send, x_recv, v_send, v_recv, m_send, m_recv, p_send, p_recv, b_send, b_recv, e_send, e_recv,
 ):
     me_i = lax.axis_index("rtile")
     me_c = lax.axis_index("stile")
     rank = v_ref.shape[-2]
     tile = v_ref.shape[-1]
-    w = x_ref.shape[-1]
+    w = x_ref.shape[-2]
     w2 = 2 * w
     count = st_ref.shape[0]
     blk = rank // 8
@@ -61,6 +61,14 @@
                     device_id_type=MESH,
                 )
 
+    loads = [
+        pltpu.make_async_copy(src, dst, in_sem.at[j])
+        for j, (src, dst) in enumerate(((x_ref, xv), (v_ref, vv), (u_ref, uv), (d_ref, dv)))
+    ]
+    for load in loads:
+        load.start()
+    load_x, load_v, load_u, load_d = loads
+
     row = lax.broadcasted_iota(jnp.int32, (rank, tile), 0)
 
     def packed(a, b, ra, rb):
@@ -68,20 +76,6 @@
         b = b.astype(F32)
         b = jnp.concatenate([b[j * blk:(j + 1) * blk] for j in reversed(range(8))], axis=0)
         return jnp.where(row < ra, a, jnp.where(row >= rank - rb, b, 0.0)).astype(BF16)
-
-    level = lax.broadcasted_iota(jnp.int32, (8, w2), 0) * blk
-    own_a = st_ref[2 * me_i]
-    own_b = st_ref[2 * me_i + 1]
-    for i in range(R):
-        ra = rk_ref[0, i, 0, own_a]
-        rb = rk_ref[0, i, 0, own_b]
-        for c in range(2):
-            vp[0, c, i * rank:(i + 1) * rank, :] = packed(
-                v_ref[0, i, 0, 0, c], v_ref[0, i, 0, 1, c], ra, rb
-            )
-        mk[0, i * 8:(i + 1) * 8, :] = (level < ra).astype(F32)
-
-    pl.semaphore_wait(barrier, R * S - 1)
 
     pending = []
 
@@ -93,28 +87,6 @@
         copy.start()
         pending.append(copy)
         return copy
-
-    v_copies = {}
-    for d in range(1, S):
-        c = lax.rem(me_c + S - d, S)
-        v_copies[d] = (
-            send(vp.at[0], vp.at[d], v_send.at[d], v_recv.at[d], me_i, c),
-            send(mk.at[0], mk.at[d], m_send.at[d], m_recv.at[d], me_i, c),
-        )
-
-    for q in range(2):
-        xs[q] = jnp.concatenate([x_ref[0, q, 0], x_ref[0, q, 1]], axis=1)
-
-    lane = lax.broadcasted_iota(jnp.int32, (1, w2), 1)
-    sgn = jnp.where(lane < w, 1.0, -1.0).astype(F32)
-
-    cell = lax.broadcasted_iota(jnp.int32, (tile, w2), 0)
-    ca = cell // EDGE
-    cb = cell % EDGE
-    has_e = (cb < EDGE - 1).astype(F32)
-    has_w = (cb > 0).astype(F32)
-    has_s = (ca < EDGE - 1).astype(F32)
-    has_n = (ca > 0).astype(F32)
 
     def one_hot(shape, edge_dim):
         e = lax.broadcasted_iota(jnp.int32, shape, edge_dim)
@@ -129,48 +101,106 @@
 
     take_edges = one_hot((4 * EDGE, tile), 0)
     put_edges = one_hot((tile, 4 * EDGE), 1)
-
-    def mask_of(d):
-        m = mk[d]
-        return jnp.broadcast_to(m[:, None, :], (R * 8, blk, w2)).reshape(R * rank, w2) > 0.5
-
-    for t in range(ITERS):
-        edge_in = (edge_in0, edge_in1)[t]
-        x0 = xs[0]
-        x1 = xs[1]
-        rhs_r = jnp.concatenate([x0, x1], axis=1).astype(BF16)
-        rhs_i = jnp.concatenate([swap(x0) * sgn, swap(x1) * sgn], axis=1).astype(BF16)
-
-        p_copies = []
-        for d in range(S):
-            if t == 0 and d:
-                for copy in v_copies[d]:
-                    copy.wait_recv()
-            both = dot(vp[d, 0], rhs_r) + dot(vp[d, 1], rhs_i)
-            pan = jnp.where(mask_of(d), both[:, :w2], both[:, w2:]).astype(BF16)
-            pan_out[t, d] = pan.reshape(R, rank, w2)
-            for k in reversed(range(R)):
-                if d or k:
-                    i = lax.rem(me_i + k, R)
-                    p_copies.append(send(
-                        pan_out.at[t, d, i], pan_in.at[t, d, me_i],
-                        p_send.at[t, d, k], p_recv.at[t, d, k],
-                        i, lax.rem(me_c + d, S),
-                    ))
-        pan_in[t, 0, me_i] = pan_out[t, 0, me_i]
-
+    lane = lax.broadcasted_iota(jnp.int32, (1, w2), 1)
+    sgn = jnp.where(lane < w, 1.0, -1.0).astype(F32)
+
+    def turned_field(v):
+        return jnp.concatenate(
+            [(swap(v[:, q * w2:(q + 1) * w2].astype(F32)) * sgn).astype(BF16) for q in range(2)], axis=1
+        )
+
+    def send_edges(t, edge_in, rhs_r):
         edges = dot(take_edges, rhs_r).astype(BF16)
         for q in range(2):
             edge_out[t, q] = edges[:, q * w2:(q + 1) * w2]
             edge_in[2 * me_i + q] = edges[:, q * w2:(q + 1) * w2]
-        e_copies = []
-        for k in range(1, R):
-            e_copies.append(send(
+        return [
+            send(
                 edge_out.at[t], edge_in.at[pl.ds(2 * me_i, 2)],
                 e_send.at[t, k], e_recv.at[t, k], lax.rem(me_i + k, R), me_c,
-            ))
+            )
+            for k in range(1, R)
+        ]
+
+    load_x.wait()
+    for q in range(2):
+        xs[q] = jnp.concatenate([xv[0, q, 0], xv[0, q, 1]], axis=0).T
+        xb[0, :, q * w2:(q + 1) * w2] = xs[q].astype(BF16)
+
+    pl.semaphore_wait(barrier, R * S - 1)
+
+    x_copies = {
+        e: send(xb.at[0], xb.at[e], x_send.at[e], x_recv.at[e], me_i, lax.rem(me_c + e, S))
+        for e in range(1, S)
+    }
+
+    level = lax.broadcasted_iota(jnp.int32, (8, w2), 0) * blk
+    own_a = st_ref[2 * me_i]
+    own_b = st_ref[2 * me_i + 1]
+    load_v.wait()
+    for i in range(R):
+        ra = rk_ref[0, i, 0, own_a]
+        rb = rk_ref[0, i, 0, own_b]
+        for c in range(2):
+            vp[0, c, i * rank:(i + 1) * rank, :] = packed(
+                vv[0, i, 0, 0, c], vv[0, i, 0, 1, c], ra, rb
+            )
+        mk[0, i * 8:(i + 1) * 8, :] = (level < ra).astype(F32)
+
+    v_copies = {}
+    for d in range(1, S):
+        c = lax.rem(me_c + S - d, S)
+        v_copies[d] = (
+            send(vp.at[0], vp.at[d], v_send.at[d], v_recv.at[d], me_i, c),
+            send(mk.at[0], mk.at[d], m_send.at[d], m_recv.at[d], me_i, c),
+        )
+
+    cell = lax.broadcasted_iota(jnp.int32, (tile, w2), 0)
+    ca = cell // EDGE
+    cb = cell % EDGE
+    has_e = (cb < EDGE - 1).astype(F32)
+    has_w = (cb > 0).astype(F32)
+    has_s = (ca < EDGE - 1).astype(F32)
+    has_n = (ca > 0).astype(F32)
+
+    def mask_of(d):
+        m = mk[d]
+        return jnp.broadcast_to(m[:, None, :], (R * 8, blk, w2)).reshape(R * rank, w2) > 0.5
+
+    for t in range(ITERS):
+        edge_in = (edge_in0, edge_in1)[t]
+        p_copies = [[] for _ in range(S)]
+        if t:
+            rhs_r = jnp.concatenate([xs[0], xs[1]], axis=1).astype(BF16)
+            rhs_i = turned_field(rhs_r)
+        for d in range(S):
+            v = 0 if t == 0 else d
+            if t == 0:
+                if d:
+                    x_copies[d].wait_recv()
+                rhs_r = xb[d]
+                rhs_i = turned_field(rhs_r)
+            both = dot(vp[v, 0], rhs_r) + dot(vp[v, 1], rhs_i)
+            pan = jnp.where(mask_of(v), both[:, :w2], both[:, w2:]).astype(BF16)
+            pan_out[t, d] = pan.reshape(R, rank, w2)
+            to = me_c if t == 0 else lax.rem(me_c + d, S)
+            for k in reversed(range(R)):
+                if k or (t and d):
+                    i = lax.rem(me_i + k, R)
+                    p_copies[d].append(send(
+                        pan_out.at[t, d, i], pan_in.at[t, d, me_i],
+                        p_send.at[t, d, k], p_recv.at[t, d, k], i, to,
+                    ))
+            if t == 0 or d == 0:
+                pan_in[t, d, me_i] = pan_out[t, d, me_i]
+            if t == 0 and d == 0:
+                e_copies = send_edges(t, edge_in, rhs_r)
+        if t:
+            e_copies = send_edges(t, edge_in, rhs_r)
 
         if t == 0:
+            load_u.wait()
+            load_d.wait()
             for p in range(R):
                 ta = st_ref[2 * p]
                 tb = st_ref[2 * p + 1]
@@ -178,18 +208,18 @@
                 rb = rk_ref[0, me_i, 0, tb]
                 for c in range(2):
                     up[c, p * rank:(p + 1) * rank, :] = packed(
-                        u_ref[0, 0, 0, ta, c], u_ref[0, 0, 0, tb, c], ra, rb
+                        uv[0, 0, 0, ta, c], uv[0, 0, 0, tb, c], ra, rb
                     )
             for s in range(S):
                 dl[s] = jnp.concatenate(
-                    [d_ref[0, 0, 0, 0, :, s * w:(s + 1) * w], d_ref[0, 0, 0, 1, :, s * w:(s + 1) * w]],
+                    [dv[0, 0, 0, 0, :, s * w:(s + 1) * w], dv[0, 0, 0, 1, :, s * w:(s + 1) * w]],
                     axis=1,
                 )
 
-        for copy in p_copies:
-            copy.wait_recv()
-        b_copies = []
+        b_copies = [[] for _ in range(S)]
         for e in range(S):
+            for copy in p_copies[e]:
+                copy.wait_recv()
             pan = pan_in[t, e].reshape(R * rank, w2)
             turned = (swap(pan.astype(F32)) * (-sgn)).astype(BF16)
             image = dot_t(up[0], pan) + dot_t(up[1], turned)
@@ -201,7 +231,7 @@
             for k in reversed(range(R)):
                 if e or k:
                     q = lax.rem(me_i + k, R)
-                    b_copies.append(send(
+                    b_copies[e].append(send(
                         back_out.at[t, e, q], back_in.at[t, e, me_i],
                         b_send.at[t, e, k], b_recv.at[t, e, k],
                         q, lax.rem(me_c + S - e, S),
@@ -217,7 +247,7 @@
             parts = []
             deg = has_e + has_w + has_s + has_n
             for side in range(4):
-                listed = nb_ref[mine, side]
+                listed = nb_ref[side, mine]
                 present = jnp.where(listed >= 0, 1.0, 0.0).astype(F32)
                 want = jnp.maximum(listed, 0)
                 slot = jnp.int32(0)
@@ -244,10 +274,13 @@
                 term = term + (x - zs[q] + us[q])
             drift.append(term)
 
-        for copy in b_copies:
-            copy.wait_recv()
         grad = jnp.zeros((tile, 2 * w2), F32)
         for d in range(S):
+            if t == 0 and d:
+                for copy in v_copies[d]:
+                    copy.wait_recv()
+            for copy in b_copies[d]:
+                copy.wait_recv()
             b = back_in[t, d].reshape(R * rank, w2).astype(F32)
             turned = swap(b) * (-sgn)
             m = mask_of(d)
@@ -266,15 +299,18 @@
                 zs[q] = z
                 us[q] = summed - z
             else:
+                xt = x.T
+                zt = z.T
                 for c in range(2):
-                    xo_ref[0, q, c] = x[:, c * w:(c + 1) * w]
-                    zo_ref[0, q, c] = z[:, c * w:(c + 1) * w]
+                    xo_ref[0, q, c] = xt[c * w:(c + 1) * w]
+                    zo_ref[0, q, c] = zt[c * w:(c + 1) * w]
 
     for copy in pending:
         copy.wait_send()
 
 
 def on_device(R, S, x_start, data, u_fac, v_fac, ranks, slot_tile, neighbours):
+    x_cells = jnp.swapaxes(x_start, -1, -2)
     w2 = 2 * x_start.shape[-1]
     tile = x_start.shape[-2]
     rank = v_fac.shape[-2]
@@ -282,14 +318,19 @@
     T = ITERS
     vmem = pl.BlockSpec(memory_space=pltpu.VMEM)
     smem = pl.BlockSpec(memory_space=pltpu.SMEM)
-    out = jax.ShapeDtypeStruct(x_start.shape, F32)
+    hbm = pl.BlockSpec(memory_space=pl.ANY)
+    out = jax.ShapeDtypeStruct(x_cells.shape, F32)
     dma = pltpu.SemaphoreType.DMA
-    return pl.pallas_call(
+    x_out, z_out = pl.pallas_call(
         functools.partial(kernel, R, S),
         out_shape=(out, out),
-        in_specs=[vmem, vmem, vmem, vmem, smem, smem, smem],
+        in_specs=[hbm, hbm, hbm, hbm, smem, smem, smem],
         out_specs=(vmem, vmem),
         scratch_shapes=[
+            pltpu.VMEM(x_cells.shape, F32),
+            pltpu.VMEM(data.shape, F32),
+            pltpu.VMEM(u_fac.shape, BF16),
+            pltpu.VMEM(v_fac.shape, BF16),
             pltpu.VMEM((S, 2, R * rank, tile), BF16),
             pltpu.VMEM((S, R * 8, w2), F32),
             pltpu.VMEM((2, R * rank, tile), BF16),
@@ -297,6 +338,7 @@
             pltpu.VMEM((slots, tile, w2), F32),
             pltpu.VMEM((slots, tile, w2), F32),
             pltpu.VMEM((slots, tile, w2), F32),
+            pltpu.VMEM((S, tile, slots * w2), BF16),
             pltpu.VMEM((T, S, R, rank, w2), BF16),
             pltpu.VMEM((T, S, R, rank, w2), BF16),
             pltpu.VMEM((T, S, R, rank, w2), BF16),
@@ -304,6 +346,7 @@
             pltpu.VMEM((T, slots, 4 * EDGE, w2), BF16),
             pltpu.VMEM((slots * R, 4 * EDGE, w2), BF16),
             pltpu.VMEM((slots * R, 4 * EDGE, w2), BF16),
+            dma((4,)), dma((S,)), dma((S,)),
             dma((S,)), dma((S,)), dma((S,)), dma((S,)),
             dma((T, S, R)), dma((T, S, R)), dma((T, S, R)), dma((T, S, R)),
             dma((T, R)), dma((T, R)),
@@ -311,7 +354,8 @@
         compiler_params=pltpu.CompilerParams(
             collective_id=0, has_side_effects=True, vmem_limit_bytes=56 * 1024 * 1024
         ),
-    )(x_start, data, u_fac, v_fac, ranks, slot_tile, neighbours)
+    )(x_cells, data, u_fac, v_fac, ranks, slot_tile, neighbours.T)
+    return jnp.swapaxes(x_out, -1, -2), jnp.swapaxes(z_out, -1, -2)
 
 
 def solution(mesh):

time: 44.9 us -> 37.9 us (0.84)
  local copies, waits for them, and re-layouts: 6.16 us -> 2.42 us
  Pallas kernels: 37.8 us -> 34.6 us
    pallas_call x1, Pallas kernels: 37.8 us -> 34.6 us  [on_device(): pl.pallas_call(functools.partial(kernel, R, S), out_shape=(out, out), in_...]
    pallas_call x2 -> x0, local copies, waits for them, and re-layouts: 2.87 us -> none  [on_device(): pl.pallas_call(functools.partial(kernel, R, S), out_shape=(out, out), in_...]
    unnamed x4, local copies, waits for them, and re-layouts: 3.29 us -> 2.42 us
where the time goes in v2:
time: 37.9 us; the launch traced here: 37.7 us
  Pallas kernels  34.6 us (91%)
  local copies, waits for them, and re-layouts  2.42 us (6%)
  between operations  0.65 us (2%)
    pallas_call x1, Pallas kernels, on_device(): pl.pallas_call(functools.partial(kernel, R, S), out_shape=(out, out), in_...  34.6 us
    unnamed x4, local copies, waits for them, and re-layouts  2.42 us

profile of v2, /device:TPU:0, one launch (start us, length us, event | category | flops | bytes accessed | tf_op | source)
XLA Modules:
  0.0 37.7 jit_solution(3850828099705009843)
XLA Ops:
  0.6 34.6 %shard_map.86 = (f32[1,2,2,64,256]{4,3,2,1,0:T(8,128)}, f32[1,2,2,64,256]{4,3,2,1,0:T(8,128)}) custom-call(f32[1,2,2,64,256]{4,3,2,1,0:T(8,128)} %bitcast.6, f32[1,1,1,2,256,128]{5,4,3,2,1,0:T(8,128)} %d_ref.1, bf16[1,1,1,8,2,64,256]{6,5,4,3,2,1,0:T(8,128)(2,1)} %u_ref.1, bf16[1,4,1,2,2,64,256]{6,5,4,3,2,1,0:T(8,128)(2,1)} %v_ref.1, s32[1,4,1,8]{3,2,1,0:T(1,128)} %rk_ref.1, ...), custom_call_target="tpu_custom_call" | custom-call | tf_op jit(solution)/shard_map/pallas_call | solution.py:324
  35.3 0.0 copy-start
  35.3 1.7 %copy.11 = f32[1,2,2,256,64]{3,4,2,1,0:T(8,128)} copy(f32[1,2,2,256,64]{3,4,2,1,0:T(8,128)} %bitcast.5) | data formatting | bytes 524288
  37.0 0.0 copy-done
  37.0 0.7 %copy.12 = f32[1,2,2,256,64]{3,4,2,1,0:T(8,128)} copy(f32[1,2,2,256,64]{3,4,2,1,0:T(8,128)S(1)} %bitcast.4) | data formatting | bytes 524288
Async XLA Ops:
  35.3 1.7 %copy-start = (f32[1,2,2,64,256]{4,3,2,1,0:T(8,128)S(1)}, f32[1,2,2,64,256]{4,3,2,1,0:T(8,128)}, u32[]{:S(2)}) copy-start(f32[1,2,2,64,256]{4,3,2,1,0:T(8,128)} %get-tuple-element.5) | copy-start | bytes 786436

commit v3 on v2

--- a/solution.py
+++ b/solution.py
@@ -37,7 +37,7 @@
 def kernel(
     R, S,
     x_ref, d_ref, u_ref, v_ref, rk_ref, st_ref, nb_ref,
-    xo_ref, zo_ref,
+    xo_ref,
     xv, dv, uv, vv, vp, mk, up, dl, xs, zs, us, xb,
     pan_out, pan_in, back_out, back_in, edge_out, edge_in0, edge_in1,
     in_sem, x_send, x_recv, v_send, v_recv, m_send, m_recv, p_send, p_recv, b_send, b_recv, e_send, e_recv,
@@ -146,14 +146,6 @@
                 vv[0, i, 0, 0, c], vv[0, i, 0, 1, c], ra, rb
             )
         mk[0, i * 8:(i + 1) * 8, :] = (level < ra).astype(F32)
-
-    v_copies = {}
-    for d in range(1, S):
-        c = lax.rem(me_c + S - d, S)
-        v_copies[d] = (
-            send(vp.at[0], vp.at[d], v_send.at[d], v_recv.at[d], me_i, c),
-            send(mk.at[0], mk.at[d], m_send.at[d], m_recv.at[d], me_i, c),
-        )
 
     cell = lax.broadcasted_iota(jnp.int32, (tile, w2), 0)
     ca = cell // EDGE
@@ -197,6 +189,15 @@
                 e_copies = send_edges(t, edge_in, rhs_r)
         if t:
             e_copies = send_edges(t, edge_in, rhs_r)
+        else:
+            v_copies = {}
+            for d in range(1, S):
+                c = lax.rem(me_c + S - d, S)
+                v_copies[d] = (
+                    send(vp.at[0], vp.at[d], v_send.at[d], v_recv.at[d], me_i, c),
+                    send(mk.at[0], mk.at[d], m_send.at[d], m_recv.at[d], me_i, c),
+                )
+
 
         if t == 0:
             load_u.wait()
@@ -302,8 +303,8 @@
                 xt = x.T
                 zt = z.T
                 for c in range(2):
-                    xo_ref[0, q, c] = xt[c * w:(c + 1) * w]
-                    zo_ref[0, q, c] = zt[c * w:(c + 1) * w]
+                    xo_ref[0, 0, q, c] = xt[c * w:(c + 1) * w]
+                    xo_ref[1, 0, q, c] = zt[c * w:(c + 1) * w]
 
     for copy in pending:
         copy.wait_send()
@@ -319,13 +320,13 @@
     vmem = pl.BlockSpec(memory_space=pltpu.VMEM)
     smem = pl.BlockSpec(memory_space=pltpu.SMEM)
     hbm = pl.BlockSpec(memory_space=pl.ANY)
-    out = jax.ShapeDtypeStruct(x_cells.shape, F32)
+    out = jax.ShapeDtypeStruct((2,) + x_cells.shape, F32)
     dma = pltpu.SemaphoreType.DMA
-    x_out, z_out = pl.pallas_call(
+    both = pl.pallas_call(
         functools.partial(kernel, R, S),
-        out_shape=(out, out),
+        out_shape=out,
         in_specs=[hbm, hbm, hbm, hbm, smem, smem, smem],
-        out_specs=(vmem, vmem),
+        out_specs=vmem,
         scratch_shapes=[
             pltpu.VMEM(x_cells.shape, F32),
             pltpu.VMEM(data.shape, F32),
@@ -355,7 +356,7 @@
             collective_id=0, has_side_effects=True, vmem_limit_bytes=56 * 1024 * 1024
         ),
     )(x_cells, data, u_fac, v_fac, ranks, slot_tile, neighbours.T)
-    return jnp.swapaxes(x_out, -1, -2), jnp.swapaxes(z_out, -1, -2)
+    return jnp.swapaxes(both[0], -1, -2), jnp.swapaxes(both[1], -1, -2)
 
 
 def solution(mesh):

time: 37.9 us -> 35.7 us (0.942)
  Pallas kernels: 34.6 us -> 33 us
  local copies, waits for them, and re-layouts: 2.42 us -> 1.85 us
    unnamed x4 -> x0, local copies, waits for them, and re-layouts: 2.42 us -> none
    transpose x0 -> x1, local copies, waits for them, and re-layouts: none -> 1.85 us  [on_device(): return (jnp.swapaxes(both[0], -1, -2), jnp.swapaxes(both[1], -1, -2))]
    pallas_call x1, Pallas kernels: 34.6 us -> 33 us  [on_device(): pl.pallas_call(functools.partial(kernel, R, S), out_shape=out, in_specs=[...]
where the time goes in v3:
time: 35.7 us; the launch traced here: 35.5 us
  Pallas kernels  33 us (92%)
  local copies, waits for them, and re-layouts  1.85 us (5%)
  between operations  0.64 us (2%)
    pallas_call x1, Pallas kernels, on_device(): pl.pallas_call(functools.partial(kernel, R, S), out_shape=out, in_specs=[...  33 us
    transpose x1, local copies, waits for them, and re-layouts, on_device(): return (jnp.swapaxes(both[0], -1, -2), jnp.swapaxes(both[1], -1, -2))  1.85 us

profile of v3, /device:TPU:0, one launch (start us, length us, event | category | flops | bytes accessed | tf_op | source)
XLA Modules:
  0.0 35.5 jit_solution(4325118510394283281)
XLA Ops:
  0.6 33.0 %shard_map.86 = f32[2,1,2,2,64,256]{5,4,3,2,1,0:T(8,128)} custom-call(f32[1,2,2,64,256]{4,3,2,1,0:T(8,128)} %bitcast.10, f32[1,1,1,2,256,128]{5,4,3,2,1,0:T(8,128)} %d_ref.1, bf16[1,1,1,8,2,64,256]{6,5,4,3,2,1,0:T(8,128)(2,1)} %u_ref.1, bf16[1,4,1,2,2,64,256]{6,5,4,3,2,1,0:T(8,128)(2,1)} %v_ref.1, s32[1,4,1,8]{3,2,1,0:T(1,128)} %rk_ref.1, s32[8]{0:T(128)} %st_ref.1, ...), custom_call_target="tpu_custom_call" | custom-call | tf_op jit(solution)/shard_map/pallas_call | solution.py:325
  33.7 1.9 %slice_bitcast_fusion = (f32[1,2,2,256,64]{3,4,2,1,0:T(8,128)}, f32[1,2,2,256,64]{3,4,2,1,0:T(8,128)}) fusion(f32[2,1,2,2,64,256]{5,4,3,2,1,0:T(8,128)} %shard_map.86), kind=kLoop, calls=%fused_computation | loop fusion | bytes 1048576 | tf_op jit(solution)/shard_map/transpose | solution.py:359

commit v4 on v3

--- a/solution.py
+++ b/solution.py
@@ -40,7 +40,7 @@
     xo_ref,
     xv, dv, uv, vv, vp, mk, up, dl, xs, zs, us, xb,
     pan_out, pan_in, back_out, back_in, edge_out, edge_in0, edge_in1,
-    in_sem, x_send, x_recv, v_send, v_recv, m_send, m_recv, p_send, p_recv, b_send, b_recv, e_send, e_recv,
+    ov, o_sem, in_sem, x_send, x_recv, v_send, v_recv, m_send, m_recv, p_send, p_recv, b_send, b_recv, e_send, e_recv,
 ):
     me_i = lax.axis_index("rtile")
     me_c = lax.axis_index("stile")
@@ -78,6 +78,7 @@
         return jnp.where(row < ra, a, jnp.where(row >= rank - rb, b, 0.0)).astype(BF16)
 
     pending = []
+    stores = []
 
     def send(src, dst, ss, rs, i, c):
         copy = pltpu.make_async_remote_copy(
@@ -303,9 +304,15 @@
                 xt = x.T
                 zt = z.T
                 for c in range(2):
-                    xo_ref[0, 0, q, c] = xt[c * w:(c + 1) * w]
-                    xo_ref[1, 0, q, c] = zt[c * w:(c + 1) * w]
-
+                    ov[0, 0, q, c] = xt[c * w:(c + 1) * w]
+                    ov[1, 0, q, c] = zt[c * w:(c + 1) * w]
+                for j in range(2):
+                    copy = pltpu.make_async_copy(ov.at[j, 0, q], xo_ref.at[j, 0, q], o_sem.at[j, q])
+                    copy.start()
+                    stores.append(copy)
+
+    for copy in stores:
+        copy.wait()
     for copy in pending:
         copy.wait_send()
 
@@ -326,7 +333,7 @@
         functools.partial(kernel, R, S),
         out_shape=out,
         in_specs=[hbm, hbm, hbm, hbm, smem, smem, smem],
-        out_specs=vmem,
+        out_specs=hbm,
         scratch_shapes=[
             pltpu.VMEM(x_cells.shape, F32),
             pltpu.VMEM(data.shape, F32),
@@ -347,6 +354,7 @@
             pltpu.VMEM((T, slots, 4 * EDGE, w2), BF16),
             pltpu.VMEM((slots * R, 4 * EDGE, w2), BF16),
             pltpu.VMEM((slots * R, 4 * EDGE, w2), BF16),
+            pltpu.VMEM((2,) + x_cells.shape, F32), dma((2, 2)),
             dma((4,)), dma((S,)), dma((S,)),
             dma((S,)), dma((S,)), dma((S,)), dma((S,)),
             dma((T, S, R)), dma((T, S, R)), dma((T, S, R)), dma((T, S, R)),

time: 35.7 us -> 35.7 us (level)
  no operation moved by 1% of the time
where the time goes in v4:
time: 35.7 us; the launch traced here: 35.5 us
  Pallas kernels  33 us (92%)
  local copies, waits for them, and re-layouts  1.85 us (5%)
  between operations  0.64 us (2%)
    pallas_call x1, Pallas kernels, on_device(): pl.pallas_call(functools.partial(kernel, R, S), out_shape=out, in_specs=[...  33 us
    transpose x1, local copies, waits for them, and re-layouts, on_device(): return (jnp.swapaxes(both[0], -1, -2), jnp.swapaxes(both[1], -1, -2))  1.85 us

profile of v4, /device:TPU:0, one launch (start us, length us, event | category | flops | bytes accessed | tf_op | source)
XLA Modules:
  0.0 35.5 jit_solution(10925616823861005144)
XLA Ops:
  0.6 33.0 %shard_map.86 = f32[2,1,2,2,64,256]{5,4,3,2,1,0:T(8,128)} custom-call(f32[1,2,2,64,256]{4,3,2,1,0:T(8,128)} %bitcast.10, f32[1,1,1,2,256,128]{5,4,3,2,1,0:T(8,128)} %d_ref.1, bf16[1,1,1,8,2,64,256]{6,5,4,3,2,1,0:T(8,128)(2,1)} %u_ref.1, bf16[1,4,1,2,2,64,256]{6,5,4,3,2,1,0:T(8,128)(2,1)} %v_ref.1, s32[1,4,1,8]{3,2,1,0:T(1,128)} %rk_ref.1, s32[8]{0:T(128)} %st_ref.1, ...), custom_call_target="tpu_custom_call" | custom-call | tf_op jit(solution)/shard_map/pallas_call | solution.py:332
  33.7 1.9 %slice_bitcast_fusion = (f32[1,2,2,256,64]{3,4,2,1,0:T(8,128)}, f32[1,2,2,256,64]{3,4,2,1,0:T(8,128)}) fusion(f32[2,1,2,2,64,256]{5,4,3,2,1,0:T(8,128)} %shard_map.86), kind=kLoop, calls=%fused_computation | loop fusion | bytes 1048576 | tf_op jit(solution)/shard_map/transpose | solution.py:367
